TPU v7x, 32 devices: a whole 2x2x4 slice. The times are simulated.
32 devices in a mesh: group: 4 (over z), shard: 8 (over y, x, core).
Axes of the slice: x: 2, y: 2, z: 4, core: 2. Of those that a mesh axis runs over, the one named last changes fastest.
Arguments:
- vectors: float32 [4096, 256], P(('group', 'shard')), may hold values from -160 to 160
- item_codes: int32 [4096], P(('group', 'shard')), may hold values from 0 to 63, as said below
- coarse_book: float32 [64, 256], replicated, may hold values from -24 to 24
- fine_books: float32 [8, 16384, 256], P('group', 'shard'), may hold values from -2 to 2
Outputs:
- item_grad: float32 [4096, 256], P(('group', 'shard'))
- fine_grad: float32 [8, 16384, 256], P('group', 'shard')
- coarse_grad: float32 [64, 256], replicated
Inputs may be any that keep to these rules, and one draw needn't show every extreme that they name: `item_codes`: the items of one device fall into one group at most 32 times, and one group receives exactly 32 items from every device.
All inputs are finite; a program needn't handle non-finite values.
Results may differ from a plain program's by a relative error of at most 0.0003.
Values sent between devices are 32-bit elements; how exact they have to be, the bound alone decides.
A program may use at most 192 MiB of HBM per device.

v0:
```python
import jax
import jax.numpy as jnp
from jax import lax
from jax.sharding import PartitionSpec as P

sharpness = 2.5
highest = lax.Precision.HIGHEST


def contract(former, latter, former_dim, latter_dim):
    return lax.dot_general(
        former,
        latter,
        (((former_dim,), (latter_dim,)), ((), ())),
        precision=highest,
        preferred_element_type=jnp.float32,
    )


def per_device(vectors, item_codes, coarse_book, fine_books):
    local_groups, book_rows, feature_count = fine_books.shape
    group_count = lax.axis_size("group")
    total_groups = local_groups * group_count
    coarse_total = coarse_book.shape[0]
    per_group = coarse_total // total_groups
    item_count = vectors.shape[0]
    slot_size = item_count // 4
    slot_total = local_groups * group_count * slot_size
    onehot = (item_codes[:, None] == jnp.arange(coarse_total, dtype=jnp.int32)[None, :]).astype(
        jnp.float32
    )
    residual = vectors - contract(onehot, coarse_book, 1, 0)
    group_of = item_codes // per_group
    member = (group_of[:, None] == jnp.arange(total_groups, dtype=jnp.int32)[None, :]).astype(
        jnp.int32
    )
    position = jnp.sum((jnp.cumsum(member, axis=0) - 1) * member, axis=1)
    target = (
        group_of % local_groups * group_count + group_of // local_groups
    ) * slot_size + position
    placing = (jnp.arange(slot_total, dtype=jnp.int32)[:, None] == target[None, :]).astype(
        jnp.float32
    )
    outgoing = contract(placing, residual, 1, 0).reshape(
        local_groups, group_count, slot_size, feature_count
    )
    occupied = jnp.sum(placing, axis=1).reshape(local_groups, group_count, slot_size)
    arrived, arrived_mask = (
        lax.all_to_all(outgoing, "group", split_axis=1, concat_axis=1, tiled=True),
        lax.all_to_all(occupied, "group", split_axis=1, concat_axis=1, tiled=True),
    )
    own_count = group_count * slot_size
    row_grads = []
    book_grads = []
    spread_rows, spread_mask = (
        lax.all_gather(arrived, "shard", axis=1, tiled=True),
        lax.all_gather(arrived_mask, "shard", axis=1, tiled=True),
    )
    row_total = spread_rows.shape[1] * slot_size
    all_rows = spread_rows.reshape(local_groups, row_total, feature_count)
    all_live = spread_mask.reshape(local_groups, row_total)
    for book_index in range(local_groups):
        codebook = fine_books[book_index]
        entries = all_rows[book_index]
        live_mask = all_live[book_index]
        scores = sharpness * contract(entries, codebook, 1, 1)
        peak_score = lax.pmax(jnp.max(scores, axis=1), "shard")
        weights = jnp.exp(scores - peak_score[:, None])
        partial_total = jnp.sum(weights, axis=1)
        partial_quant = contract(weights, codebook, 1, 0)
        quant_sum, denominator = lax.psum((partial_quant, partial_total), "shard")
        quantized = quant_sum / denominator[:, None]
        error_rows = (quantized - entries) * live_mask[:, None]
        inner_term = jnp.sum(error_rows * quantized, axis=1)
        own_error = lax.dynamic_slice_in_dim(
            error_rows, lax.axis_index("shard") * own_count, own_count, 0
        )
        probability = weights / denominator[:, None]
        alignment = contract(error_rows, codebook, 1, 1)
        slopes = probability * (alignment - inner_term[:, None])
        pushed = sharpness * contract(slopes, codebook, 1, 0)
        back_sum = lax.psum_scatter(pushed, "shard", scatter_dimension=0, tiled=True)
        row_grads.append(back_sum - own_error)
        book_grads.append(
            contract(probability, error_rows, 0, 0) + sharpness * contract(slopes, entries, 0, 0)
        )
    fine_grad = jnp.stack(book_grads)
    returned = jnp.stack(row_grads).reshape(local_groups, group_count, slot_size, feature_count)
    homeward = lax.all_to_all(returned, "group", split_axis=1, concat_axis=1, tiled=True)
    item_grad = contract(placing, homeward.reshape(slot_total, feature_count), 0, 0)
    coarse_grad = lax.psum(-contract(onehot, item_grad, 0, 0), ("group", "shard"))
    return (item_grad, fine_grad, coarse_grad)


def solution(mesh):
    placed = (P(("group", "shard"), None), P(("group", "shard")), P(), P("group", "shard", None))
    return jax.shard_map(
        per_device,
        mesh=mesh,
        in_specs=placed,
        out_specs=(P(("group", "shard"), None), P("group", "shard", None), P()),
        check_vma=False,
    )
```

profile of v0, /device:TPU:1, one launch (start us, length us, event | category | flops | bytes accessed | tf_op | source)
XLA Modules:
  0.0 424.2 jit_solution(4218361691198343421)
XLA Ops:
  9.0 1.2 convolution_subtract_fusion
  10.5 12.2 %all_to_all.15 = f32[2,4,32,256]{3,2,0,1:T(8,128)} all-to-all(f32[2,4,32,256]{3,2,0,1:T(8,128)S(1)} %copy.20), channel_id=1, replica_groups=mesh['group'=4,'shard'=8] {'group'}, dimensions={1} | all-to-all | bytes 524288 | tf_op jit(solution)/shard_map/all_to_all | solution.py:49
  23.5 4.2 %all-to-all-start.1 = ((f32[2,4,32]{2,0,1:T(2,128)}), f32[2,4,32]{2,0,1:T(2,128)S(1)}, u32[]{:S(2)}, u32[]{:S(2)}) async-start(f32[2,4,32]{2,0,1:T(2,128)} %copy.21), calls=%async_computation.1 | async-start | bytes 8192 | tf_op jit(solution)/shard_map/all_to_all | solution.py:50
  27.8 4.4 %all-to-all-done.1 = f32[2,4,32]{2,0,1:T(2,128)S(1)} async-done(((f32[2,4,32]{2,0,1:T(2,128)}), f32[2,4,32]{2,0,1:T(2,128)S(1)}, u32[]{:S(2)}, u32[]{:S(2)}) %all-to-all-start.1) | async-done | bytes 1056 | tf_op jit(solution)/shard_map/all_to_all | solution.py:50
  32.2 11.9 %all_gather.7 = f32[2,32,32]{2,0,1:T(2,128)S(1)} all-gather(f32[2,4,32]{2,0,1:T(2,128)S(1)} %all-to-all-done.1), channel_id=1, replica_groups=mesh['group'=4,'shard'=8] {'shard'}, dimensions={1}, use_global_device_ids=true | all-gather | bytes 9216 | tf_op jit(solution)/shard_map/all_gather | solution.py:57
  44.4 8.3 %all-gather.2.cloned.1.call-done = f32[2,32,32,256]{3,2,0,1:T(8,128)} async-done(((f32[2,4,32,256]{3,2,0,1:T(8,128)}), f32[2,32,32,256]{3,2,0,1:T(8,128)}) %all-gather.2.cloned.1.call-update) | async-done | bytes 2097168 | tf_op jit(solution)/shard_map/all_gather | solution.py:56
  52.7 1.7 fusion.55
  54.4 10.6 %multiply_reduce_fusion = (f32[1024]{0:T(1024)S(1)}, f32[1024,2048]{1,0:T(8,128)}) fusion(f32[1024,256]{1,0:T(8,128)S(1)} %bitcast.62, f32[2,2048,256]{2,1,0:T(8,128)} %param.7), kind=kOutput, calls=%fused_computation.4 | convolution fusion | flops 6446644224 | bytes 11538432 | tf_op jit(solution)/shard_map/dot_general | solution.py:11
  65.0 9.2 %multiply_reduce_fusion.1 = (f32[1024]{0:T(1024)S(1)}, f32[1024,2048]{1,0:T(8,128)}) fusion(f32[1024,256]{1,0:T(8,128)S(1)} %bitcast.60, f32[2,2048,256]{2,1,0:T(8,128)S(1)} %copy-done.4), kind=kOutput, calls=%fused_computation.5 | convolution fusion | flops 6446644224 | bytes 11538432 | tf_op jit(solution)/shard_map/dot_general | solution.py:11
  74.2 11.8 %all-reduce.2 = (f32[1024]{0:T(1024)S(1)}, f32[1024]{0:T(1024)S(1)}) all-reduce(f32[1024]{0:T(1024)S(1)} %get-tuple-element.17, f32[1024]{0:T(1024)S(1)} %get-tuple-element.19), channel_id=1, replica_groups=mesh['group'=4,'shard'=8] {'shard'}, use_global_device_ids=true, to_apply=%region_11.12 | all-reduce | flops 2048 | bytes 16384 | tf_op jit(solution)/shard_map/pmax | solution.py:67
  86.0 11.6 %fusion.3 = f32[1024,256]{1,0:T(8,128)} fusion(f32[1024,2048]{1,0:T(8,128)} %get-tuple-element.18, f32[1024]{0:T(1024)S(1)} %get-tuple-element.9, f32[2,2048,256]{2,1,0:T(8,128)} %param.7), kind=kOutput, calls=%fused_computation.9 | convolution fusion | flops 6446645248 | bytes 11538432 | tf_op jit(solution)/shard_map/dot_general | solution.py:11
  97.6 8.3 %fusion = f32[1024,256]{1,0:T(8,128)} fusion(f32[1024,2048]{1,0:T(8,128)S(1)} %copy-done.3, f32[1024]{0:T(1024)S(1)} %get-tuple-element.10, f32[2,2048,256]{2,1,0:T(8,128)S(1)} %copy-done.5), kind=kOutput, calls=%fused_computation.6 | convolution fusion | flops 6446645248 | bytes 11538432 | tf_op jit(solution)/shard_map/dot_general | solution.py:11
  106.3 4.4 %fusion.5 = f32[1024]{0:T(1024)S(1)} fusion(f32[1024,2048]{1,0:T(8,128)} %get-tuple-element.18, f32[1024]{0:T(1024)S(1)} %get-tuple-element.9), kind=kLoop, calls=%fused_computation.11 | loop fusion | flops 6290432 | bytes 8396800 | tf_op jit(solution)/shard_map/reduce_sum | solution.py:69
  110.7 4.7 %fusion.2 = f32[1024]{0:T(1024)S(1)} fusion(f32[1024,2048]{1,0:T(8,128)} %get-tuple-element.20, f32[1024]{0:T(1024)S(1)} %get-tuple-element.10), kind=kLoop, calls=%fused_computation.8 | loop fusion | flops 6290432 | bytes 8396800 | tf_op jit(solution)/shard_map/reduce_sum | solution.py:69
  115.4 13.4 %all-reduce = (f32[1024]{0:T(1024)S(1)}, f32[1024]{0:T(1024)S(1)}) all-reduce(f32[1024]{0:T(1024)S(1)} %fusion.5, f32[1024]{0:T(1024)S(1)} %fusion.2), channel_id=1, replica_groups=mesh['group'=4,'shard'=8] {'shard'}, use_global_device_ids=true, to_apply=%region_13.14 | all-reduce | flops 2048 | bytes 16384 | tf_op jit(solution)/shard_map/psum | solution.py:71
  128.8 39.2 %all-reduce.8.cloned.1.call-done = (f32[1024,256]{1,0:T(8,128)}, f32[1024,256]{1,0:T(8,128)}) async-done(((f32[1024,256]{1,0:T(8,128)}, f32[1024,256]{1,0:T(8,128)}), (f32[1024,256]{1,0:T(8,128)}, f32[1024,256]{1,0:T(8,128)})) %all-reduce.8.cloned.1.call-update) | async-done | bytes 2097168 | tf_op jit(solution)/shard_map/psum | solution.py:71
  168.0 2.4 multiply_reduce_fusion.2
  170.4 12.2 %subtract_multiply_fusion = f32[1024,2048]{1,0:T(8,128)S(1)} fusion(f32[1024,256]{1,0:T(8,128)S(1)} %get-tuple-element.14, f32[1024]{0:T(1024)S(1)} %get-tuple-element.13, f32[2,2048,256]{2,1,0:T(8,128)} %param.7, f32[1024]{0:T(1024)S(1)} %get-tuple-element.5, f32[1024]{0:T(1024)S(1)} %get-tuple-element.9, f32[1024,2048]{1,0:T(8,128)} %get-tuple-element.18), kind=kOutput, calls=%fused_computation | convolution fusion | flops 6452936704 | bytes 19935232 | tf_op jit(solution)/shard_map/dot_general | solution.py:11
  182.6 3.2 copy-done.2
  185.8 7.7 %fusion.37 = f32[1024,256]{1,0:T(8,128)} fusion(f32[1024,2048]{1,0:T(8,128)S(1)} %subtract_multiply_fusion, f32[2,2048,256]{2,1,0:T(8,128)S(1)} %copy-done.6), kind=kOutput, calls=%fused_computation.44 | convolution fusion | flops 6442713088 | bytes 11534336 | tf_op jit(solution)/shard_map/dot_general | solution.py:11
  193.5 12.1 %subtract_multiply_fusion.1 = f32[1024,2048]{1,0:T(8,128)S(1)} fusion(f32[1024,256]{1,0:T(8,128)S(1)} %get-tuple-element.22, f32[1024]{0:T(1024)S(1)} %get-tuple-element.21, f32[2,2048,256]{2,1,0:T(8,128)} %param.7, f32[1024]{0:T(1024)S(1)} %get-tuple-element.6, f32[1024]{0:T(1024)S(1)} %get-tuple-element.10, f32[1024,2048]{1,0:T(8,128)} %get-tuple-element.20), kind=kOutput, calls=%fused_computation.2 | convolution fusion | flops 6452936704 | bytes 19935232 | tf_op jit(solution)/shard_map/dot_general | solution.py:11
  205.6 3.2 copy-done.1
  208.8 7.6 %fusion.34 = f32[1024,256]{1,0:T(8,128)} fusion(f32[1024,2048]{1,0:T(8,128)S(1)} %subtract_multiply_fusion.1, f32[2,2048,256]{2,1,0:T(8,128)S(1)} %copy-done.7), kind=kOutput, calls=%fused_computation.43 | convolution fusion | flops 6442713088 | bytes 11534336 | tf_op jit(solution)/shard_map/dot_general | solution.py:11
  216.5 18.2 %fusion.51 = f32[2048,256]{1,0:T(8,128)} fusion(f32[1024,256]{1,0:T(8,128)} %copy-done.9, f32[1024,2048]{1,0:T(8,128)} %get-tuple-element.18, f32[1024]{0:T(1024)S(1)} %get-tuple-element.5, f32[1024]{0:T(1024)S(1)} %get-tuple-element.9), kind=kOutput, calls=%fused_computation.84 | convolution fusion | flops 6448742400 | bytes 11542528 | tf_op jit(solution)/shard_map/dot_general | solution.py:11
  234.7 17.1 %fusion.13 = f32[1,2048,256]{2,1,0:T(8,128)} fusion(f32[2048,256]{1,0:T(8,128)} %fusion.51, f32[1024,2048]{1,0:T(8,128)} %copy-done.2, f32[1024,256]{1,0:T(8,128)S(1)} %bitcast.63), kind=kOutput, calls=%fused_computation.22 | convolution fusion | flops 6443499520 | bytes 13631488 | tf_op jit(solution)/shard_map/dot_general | solution.py:11
  251.8 18.2 %fusion.53 = f32[2048,256]{1,0:T(8,128)} fusion(f32[1024,256]{1,0:T(8,128)S(1)} %get-tuple-element.22, f32[1024,2048]{1,0:T(8,128)} %get-tuple-element.20, f32[1024]{0:T(1024)S(1)} %get-tuple-element.6, f32[1024]{0:T(1024)S(1)} %get-tuple-element.10), kind=kOutput, calls=%fused_computation.85 | convolution fusion | flops 6448742400 | bytes 11542528 | tf_op jit(solution)/shard_map/dot_general | solution.py:11
  270.0 1.0 dynamic-slice_subtract_fusion
  272.7 4.3 %all-to-all-start.2 = ((f32[2,4,32,256]{3,2,0,1:T(8,128)}), f32[2,4,32,256]{3,2,0,1:T(8,128)S(1)}, u32[]{:S(2)}, u32[]{:S(2)}) async-start(f32[2,4,32,256]{3,2,0,1:T(8,128)} %pad_maximum_fusion.1), calls=%async_computation.4 | async-start | bytes 524288 | tf_op jit(solution)/shard_map/all_to_all | solution.py:89
  277.0 17.2 %fusion.11 = f32[1,2048,256]{2,1,0:T(8,128)} fusion(f32[2048,256]{1,0:T(8,128)} %fusion.53, f32[1024,2048]{1,0:T(8,128)} %copy-done.1, f32[1024,256]{1,0:T(8,128)S(1)} %bitcast.61), kind=kOutput, calls=%fused_computation.20 | convolution fusion | flops 6443499520 | bytes 13631488 | tf_op jit(solution)/shard_map/dot_general | solution.py:11
  295.6 3.9 pad_maximum_fusion
  299.4 116.6 %all-reduce.6.cloned.1.call-done = f32[64,256]{1,0:T(8,128)} async-done(((f32[64,256]{1,0:T(8,128)}), f32[64,256]{1,0:T(8,128)}) %all-reduce.6.cloned.1.call-update) | async-done | bytes 65552 | tf_op jit(solution)/shard_map/psum | solution.py:91
  416.0 1.5 copy.28
  (53 shorter events, 6.7 us)
Async XLA Ops:
  7.2 1.9 copy-start
  7.2 45.5 %all-gather.2.cloned.1.call-start = ((), (), s32[]{:S(2)}) async-start(), calls=%async_computation.5 | async-start | bytes 2359296 | tf_op jit(solution)/shard_map/all_gather | solution.py:56
  23.5 8.7 %all-to-all-start.1 = ((f32[2,4,32]{2,0,1:T(2,128)}), f32[2,4,32]{2,0,1:T(2,128)S(1)}, u32[]{:S(2)}, u32[]{:S(2)}) async-start(f32[2,4,32]{2,0,1:T(2,128)} %copy.21), calls=%async_computation.1 | async-start | bytes 8192 | tf_op jit(solution)/shard_map/all_to_all | solution.py:50
  27.8 140.2 %all-reduce.8.cloned.1.call-start = ((), (), s32[]{:S(2)}) async-start(), calls=%async_computation.9 | async-start | bytes 4194304 | tf_op jit(solution)/shard_map/psum | solution.py:71
  54.4 10.6 %copy-start.4 = (f32[2,2048,256]{2,1,0:T(8,128)S(1)}, f32[2,2048,256]{2,1,0:T(8,128)}, u32[]{:S(2)}) copy-start(f32[2,2048,256]{2,1,0:T(8,128)} %param.7) | copy-start | bytes 12582916
  86.0 11.6 %copy-start.3 = (f32[1024,2048]{1,0:T(8,128)S(1)}, f32[1024,2048]{1,0:T(8,128)}, u32[]{:S(2)}) copy-start(f32[1024,2048]{1,0:T(8,128)} %get-tuple-element.20) | copy-start | bytes 25165828
  86.0 11.6 %copy-start.5 = (f32[2,2048,256]{2,1,0:T(8,128)S(1)}, f32[2,2048,256]{2,1,0:T(8,128)}, u32[]{:S(2)}) copy-start(f32[2,2048,256]{2,1,0:T(8,128)} %param.7) | copy-start | bytes 12582916
  105.9 164.2 %reduce-scatter.5.cloned.1.call-start = ((), (), s32[]{:S(2)}) async-start(), calls=%async_computation.7 | async-start | bytes 1179648 | tf_op jit(solution)/shard_map/reduce_scatter | solution.py:82
  170.4 12.2 %copy-start.9 = (f32[1024,256]{1,0:T(8,128)}, f32[1024,256]{1,0:T(8,128)S(1)}, u32[]{:S(2)}) copy-start(f32[1024,256]{1,0:T(8,128)S(1)} %get-tuple-element.14) | copy-start | bytes 3145732
  170.4 15.4 %copy-start.6 = (f32[2,2048,256]{2,1,0:T(8,128)S(1)}, f32[2,2048,256]{2,1,0:T(8,128)}, u32[]{:S(2)}) copy-start(f32[2,2048,256]{2,1,0:T(8,128)} %param.7) | copy-start | bytes 12582916
  182.6 3.2 copy-start.2
  193.5 77.5 %reduce-scatter.3.cloned.1.call-start = ((), (), s32[]{:S(2)}) async-start(), calls=%async_computation.6 | async-start | bytes 1179648 | tf_op jit(solution)/shard_map/reduce_scatter | solution.py:82
  193.5 15.3 %copy-start.7 = (f32[2,2048,256]{2,1,0:T(8,128)S(1)}, f32[2,2048,256]{2,1,0:T(8,128)}, u32[]{:S(2)}) copy-start(f32[2,2048,256]{2,1,0:T(8,128)} %param.7) | copy-start | bytes 12582916
  205.6 3.2 copy-start.1
  272.7 21.6 %all-to-all-start.2 = ((f32[2,4,32,256]{3,2,0,1:T(8,128)}), f32[2,4,32,256]{3,2,0,1:T(8,128)S(1)}, u32[]{:S(2)}, u32[]{:S(2)}) async-start(f32[2,4,32,256]{3,2,0,1:T(8,128)} %pad_maximum_fusion.1), calls=%async_computation.4 | async-start | bytes 524288 | tf_op jit(solution)/shard_map/all_to_all | solution.py:89
  277.0 17.6 %copy-start.11 = (s32[128]{0:T(128)S(1)}, s32[128]{0:T(128)}, u32[]{:S(2)}) copy-start(s32[128]{0:T(128)} %param.5) | copy-start | bytes 1540
  277.0 18.6 %copy-start.8 = (f32[1,2048,256]{2,1,0:T(8,128)S(1)}, f32[1,2048,256]{2,1,0:T(8,128)}, u32[]{:S(2)}) copy-start(f32[1,2048,256]{2,1,0:T(8,128)} %fusion.13) | copy-start | bytes 6291460
  277.0 139.0 %all-reduce.6.cloned.1.call-start = ((), (), s32[]{:S(2)}) async-start(), calls=%async_computation.8 | async-start | bytes 131072 | tf_op jit(solution)/shard_map/psum | solution.py:91
  294.6 122.9 %copy-start.10 = (f32[128,256]{1,0:T(8,128)}, f32[128,256]{1,0:T(8,128)S(1)}, u32[]{:S(2)}) copy-start(f32[128,256]{1,0:T(8,128)S(1)} %fusion.40) | copy-start | bytes 393220
Sparse Core Ops, SparseCore 0:
  22.9 29.7 all-gather.1
  106.0 61.9 all-reduce.7
  193.6 36.1 reduce-scatter.4
  234.8 36.1 reduce-scatter.2
  295.7 120.3 all-reduce.5
where the time goes:
time: 432 us; the launch traced here: 424 us
  waiting for transfers between devices  169 us (39%)
  matrix products  153 us (35%)
  blocking collectives  49.3 us (11%)
  other arithmetic  19.8 us (5%)
  between operations  14.2 us (3%)
  local copies, waits for them, and re-layouts  10.6 us (2%)
  starting transfers between devices  9.12 us (2%)
    dot_general x16, matrix products, contract(): lax.dot_general(former, latter, (((former_dim,), (latter_dim,)), ((), ())...  153 us
    psum x1, waiting for transfers between devices, per_device(): lax.psum(-contract(onehot, item_grad, 0, 0), ('group', 'shard'))  117 us
    psum x1, waiting for transfers between devices, per_device(): quant_sum, denominator = lax.psum((partial_quant, partial_total), 'shard')  39.2 us
    psum x1, blocking collectives, per_device(): quant_sum, denominator = lax.psum((partial_quant, partial_total), 'shard')  13.4 us
    all_to_all x1, blocking collectives, per_device(): lax.all_to_all(outgoing, 'group', split_axis=1, concat_axis=1, tiled=True)  12.2 us
    all_gather x1, blocking collectives, per_device(): lax.all_gather(arrived_mask, 'shard', axis=1, tiled=True)  11.9 us
    pmax x1, blocking collectives, per_device(): peak_score = lax.pmax(jnp.max(scores, axis=1), 'shard')  11.8 us
    reduce_sum x2, other arithmetic, per_device(): partial_total = jnp.sum(weights, axis=1)  9.09 us
  transfers between devices with their start and end apart: 7, of which 4 were waited for; matrix products, arithmetic and copies ran while one was open for 25% of the time, Pallas kernels for 0%

commit v1 on v0

v1 whole, which is shorter than its diff:
```python
import functools

import jax
import jax.numpy as jnp
from jax import lax
from jax.experimental import pallas as pl
from jax.experimental.pallas import tpu as pltpu
from jax.sharding import PartitionSpec as P

sharpness = 2.5
highest = lax.Precision.HIGHEST
MESH = pl.DeviceIdType.MESH
VACANT = 4096.0
STAT = 8


def contract(former, latter, former_dim, latter_dim):
    return lax.dot_general(
        former,
        latter,
        (((former_dim,), (latter_dim,)), ((), ())),
        precision=highest,
        preferred_element_type=jnp.float32,
    )


def halves(value):
    high = value.astype(jnp.bfloat16)
    return high, (value - high.astype(jnp.float32)).astype(jnp.bfloat16)


def triple(former, latter, latter_dim):
    def one(left, right):
        return lax.dot_general(
            left,
            right,
            (((1,), (latter_dim,)), ((), ())),
            preferred_element_type=jnp.float32,
        )

    return (
        one(former[0], latter[0]) + one(former[0], latter[1]) + one(former[1], latter[0])
    )


def kernel(
    group_count,
    shard_count,
    slot,
    chunk,
    outgoing,
    books,
    home_out,
    fine_t,
    rows,
    book_high,
    book_low,
    weight_high,
    weight_low,
    scores,
    part_in,
    part_out,
    full,
    back,
    home,
    z_send,
    z_recv,
    ag_send,
    ag_recv,
    q_send,
    q_recv,
    f_send,
    f_recv,
    b_send,
    b_recv,
    h_send,
    h_recv,
):
    local_groups, book_rows, width = books.shape
    own = group_count * slot
    chips = shard_count // 2
    g = lax.axis_index("group")
    s = lax.axis_index("shard")
    chip = s // 2

    def shard_peer(offset):
        return lax.rem(s + offset, shard_count)

    def group_peer(offset):
        return lax.rem(g + offset, group_count)

    def remote(src, dst, send, recv, where):
        return pltpu.make_async_remote_copy(
            src_ref=src,
            dst_ref=dst,
            send_sem=send,
            recv_sem=recv,
            device_id=where,
            device_id_type=MESH,
        )

    barrier = pltpu.get_barrier_semaphore()
    for offset in range(1, group_count):
        pl.semaphore_signal(barrier, inc=1, device_id=(group_peer(offset), s), device_id_type=MESH)
    for offset in range(1, shard_count):
        pl.semaphore_signal(barrier, inc=1, device_id=(g, shard_peer(offset)), device_id_type=MESH)
    pl.semaphore_wait(barrier, group_count + shard_count - 2)

    def z_copy(b, other, landing):
        return remote(
            outgoing.at[b, other],
            rows.at[b, s, pl.ds(landing * slot, slot)],
            z_send.at[b, other],
            z_recv.at[b, landing],
            (other, s),
        )

    for b in range(local_groups):
        for offset in range(1, group_count):
            z_copy(b, group_peer(offset), g).start()
        rows[b, s, pl.ds(g * slot, slot)] = outgoing[b, g]

    def ag_copy(b, other, block):
        return remote(
            rows.at[b, block], rows.at[b, block], ag_send.at[b, other], ag_recv.at[b, block], (g, other)
        )

    def spread_rows(b):
        for offset in range(1, group_count):
            z_copy(b, group_peer(offset), group_peer(offset)).wait_recv()
        for offset in range(1, shard_count):
            other = shard_peer(offset)
            ag_copy(b, other, s).start()

    @pl.loop(0, book_rows // chunk)
    def _(step):
        at = pl.ds(step * chunk, chunk)
        for b in range(local_groups):
            high, low = halves(books[b, at])
            book_high[b, at] = high
            book_low[b, at] = low

    for b in range(local_groups):
        spread_rows(b)

    def load_rows(b, at, count):
        value = rows[b, at].reshape(count, width)
        live = (value[:, :1] < VACANT / 2).astype(jnp.float32)
        return value * live, live

    def book(b, step):
        at = pl.ds(step * chunk, chunk)
        return book_high[b, at], book_low[b, at]

    def q_copy(b, other, sender):
        return remote(
            part_out.at[b, other], part_in.at[b, sender], q_send.at[b, other], q_recv.at[b, sender], (g, other)
        )

    def b_copy(b, other, sender):
        return remote(
            part_out.at[b, other, pl.ds(0, own)],
            part_in.at[b, sender, pl.ds(0, own)],
            b_send.at[b, other],
            b_recv.at[b, sender],
            (g, other),
        )

    def f_copy(b, other, block):
        return remote(
            full.at[b, block], full.at[b, block], f_send.at[b, other], f_recv.at[b, block], (g, other)
        )

    steps = book_rows // chunk

    def score_tile(b, turn):
        tile = lax.rem(chip + turn, chips)
        for core in range(2):
            owner = 2 * tile + core

            @pl.when(owner != s)
            def _():
                ag_copy(b, owner, owner).wait_recv()

        entries, _ = load_rows(b, pl.ds(2 * tile, 2), 2 * own)
        pair = halves(entries)
        peak = None
        for step in range(steps):
            value = sharpness * triple(pair, book(b, step), 1)
            scores[:, step * chunk : (step + 1) * chunk] = value
            top = jnp.max(value, axis=1, keepdims=True)
            peak = top if peak is None else jnp.maximum(peak, top)
        total = jnp.zeros((2 * own, 1), jnp.float32)
        quant = jnp.zeros((2 * own, width), jnp.float32)
        for step in range(steps):
            weight = jnp.exp(scores[:, step * chunk : (step + 1) * chunk] - peak)
            total += jnp.sum(weight, axis=1, keepdims=True)
            high, low = halves(weight)
            weight_high[b, tile, :, step * chunk : (step + 1) * chunk] = high
            weight_low[b, tile, :, step * chunk : (step + 1) * chunk] = low
            quant += triple((high, low), book(b, step), 0)
        lane = lax.broadcasted_iota(jnp.int32, (2 * own, 128), 1)
        stats = jnp.where(lane == 0, peak, total)
        for core in range(2):
            owner = 2 * tile + core
            part_out[b, owner, :own] = quant[core * own : (core + 1) * own]
            part_out[b, owner, own:, :own] = stats[core * own : (core + 1) * own].T[:STAT]

            @pl.when(owner != s)
            def _():
                q_copy(b, owner, s).start()

    def combine(b):
        for offset in range(1, shard_count):
            q_copy(b, shard_peer(offset), shard_peer(offset)).wait_recv()
        part_in[b, s] = part_out[b, s]
        peaks = jnp.concatenate([part_in[b, i, own : own + 1, :own] for i in range(shard_count)], axis=0)
        totals = jnp.concatenate(
            [part_in[b, i, own + 1 : own + 2, :own] for i in range(shard_count)], axis=0
        )
        peak = jnp.max(peaks, axis=0, keepdims=True)
        factor = jnp.exp(peaks - peak)
        total = jnp.sum(factor * totals, axis=0, keepdims=True)
        factor_t = (factor / total).T
        value = jnp.zeros((own, width), jnp.float32)
        for i in range(shard_count):
            value += factor_t[:, i : i + 1] * part_in[b, i, :own]
        full[b, s, :own] = value
        line = lax.broadcasted_iota(jnp.int32, (STAT, own), 0)
        full[b, s, own:, :own] = jnp.where(line == 0, peak, 1.0 / total)
        for offset in range(1, shard_count):
            f_copy(b, shard_peer(offset), s).start()

    def slope_tile(b, turn):
        tile = lax.rem(chip + turn, chips)
        columns = []
        for core in range(2):
            owner = 2 * tile + core

            @pl.when(owner != s)
            def _():
                f_copy(b, owner, owner).wait_recv()
                q_copy(b, owner, s).wait_send()

            mine = part_out[b, owner, own:, :own]
            whole = full[b, owner, own:, :own]
            columns.append((jnp.exp(mine[:1] - whole[:1]) * whole[1:2] + jnp.zeros_like(mine)).T[:, :1])
        alpha = jnp.concatenate(columns, axis=0)
        entries, live = load_rows(b, pl.ds(2 * tile, 2), 2 * own)
        quantized = jnp.concatenate([full[b, 2 * tile, :own], full[b, 2 * tile + 1, :own]], axis=0)
        error = (quantized - entries) * live
        inner = jnp.sum(error * quantized, axis=1, keepdims=True)
        error_pair = halves(error)
        error_t = halves((alpha * error).T)
        entries_t = halves((sharpness * alpha * entries).T)
        pushed = jnp.zeros((2 * own, width), jnp.float32)
        for step in range(steps):
            at = slice(step * chunk, (step + 1) * chunk)
            align = triple(error_pair, book(b, step), 1)
            high = weight_high[b, tile, :, at]
            low = weight_low[b, tile, :, at]
            slope = (high.astype(jnp.float32) + low.astype(jnp.float32)) * (align - inner)
            slope_pair = halves(slope)
            pushed += triple(slope_pair, book(b, step), 0)
            fine_t[b, :, at] += triple(error_t, (high, low), 0) + triple(entries_t, slope_pair, 0)
        pushed = sharpness * alpha * pushed
        for core in range(2):
            owner = 2 * tile + core
            part_out[b, owner, :own] = pushed[core * own : (core + 1) * own]

            @pl.when(owner != s)
            def _():
                b_copy(b, owner, s).start()

    def h_copy(b, other, landing):
        return remote(
            back.at[b, other], home.at[b, landing], h_send.at[b, other], h_recv.at[b, landing], (other, s)
        )

    def finish(b):
        for offset in range(1, shard_count):
            b_copy(b, shard_peer(offset), shard_peer(offset)).wait_recv()
        entries, live = load_rows(b, pl.ds(s, 1), own)
        value = part_out[b, s, :own] - (full[b, s, :own] - entries) * live
        for offset in range(1, shard_count):
            value += part_in[b, shard_peer(offset), :own]
        back[b] = value.reshape(group_count, slot, width)
        for offset in range(1, group_count):
            h_copy(b, group_peer(offset), g).start()
        home[b, g] = back[b, g]

    def score_tiles(b, first, last):
        @pl.loop(first, last)
        def _(turn):
            score_tile(b, turn)

    def slope_tiles(b, first, last):
        @pl.loop(first, last)
        def _(turn):
            slope_tile(b, turn + 1)

    fine_t[...] = jnp.zeros_like(fine_t)
    half = chips // 2
    score_tiles(0, 0, chips)
    for b in range(1, local_groups):
        score_tiles(b, 0, half)
        combine(b - 1)
        score_tiles(b, half, chips)
    if local_groups == 1:
        combine(0)
    for b in range(local_groups):
        slope_tiles(b, 0, half)
        if b == 0 and local_groups > 1:
            combine(local_groups - 1)
        if b > 0:
            finish(b - 1)
        slope_tiles(b, half, chips)
    finish(local_groups - 1)
    for b in range(local_groups):
        for offset in range(1, group_count):
            h_copy(b, group_peer(offset), group_peer(offset)).wait_recv()
    home_out[...] = home[...]
    for b in range(local_groups):
        for offset in range(1, group_count):
            h_copy(b, group_peer(offset), g).wait_send()
            z_copy(b, group_peer(offset), g).wait_send()
        for offset in range(1, shard_count):
            other = shard_peer(offset)
            ag_copy(b, other, s).wait_send()
            f_copy(b, other, s).wait_send()
            b_copy(b, other, s).wait_send()


def per_device(vectors, item_codes, coarse_book, fine_books):
    local_groups, book_rows, width = fine_books.shape
    group_count = lax.axis_size("group")
    shard_count = lax.axis_size("shard")
    total_groups = local_groups * group_count
    coarse_total = coarse_book.shape[0]
    per_group = coarse_total // total_groups
    item_count = vectors.shape[0]
    slot = item_count // 4
    slot_total = total_groups * slot
    own = group_count * slot
    chunk = min(512, book_rows)
    onehot = (item_codes[:, None] == jnp.arange(coarse_total, dtype=jnp.int32)[None, :]).astype(
        jnp.float32
    )
    residual = vectors - contract(onehot, coarse_book, 1, 0)
    group_of = item_codes // per_group
    member = (group_of[:, None] == jnp.arange(total_groups, dtype=jnp.int32)[None, :]).astype(
        jnp.float32
    )
    index = jnp.arange(item_count, dtype=jnp.int32)
    earlier = (index[:, None] > index[None, :]).astype(jnp.float32)
    position = jnp.sum(contract(earlier, member, 1, 0) * member, axis=1).astype(jnp.int32)
    target = (
        group_of % local_groups * group_count + group_of // local_groups
    ) * slot + position
    placing = (jnp.arange(slot_total, dtype=jnp.int32)[:, None] == target[None, :]).astype(
        jnp.float32
    )
    vacant = VACANT * (1.0 - jnp.sum(placing, axis=1, keepdims=True))
    outgoing = (contract(placing, residual, 1, 0) + vacant).reshape(
        local_groups, group_count, slot, width
    )
    f32, bf16 = jnp.float32, jnp.bfloat16
    dma = pltpu.SemaphoreType.DMA
    message = (local_groups, shard_count, own + STAT, width)
    weights = (local_groups, shard_count // 2, 2 * own, book_rows)
    vmem = pl.BlockSpec(memory_space=pltpu.VMEM)
    home, fine_t = pl.pallas_call(
        functools.partial(kernel, group_count, shard_count, slot, chunk),
        out_shape=(
            jax.ShapeDtypeStruct((local_groups, group_count, slot, width), f32),
            jax.ShapeDtypeStruct((local_groups, width, book_rows), f32),
        ),
        in_specs=[vmem, vmem],
        out_specs=(vmem, vmem),
        scratch_shapes=[
            pltpu.VMEM((local_groups, shard_count, own, width), f32),
            pltpu.VMEM((local_groups, book_rows, width), bf16),
            pltpu.VMEM((local_groups, book_rows, width), bf16),
            pltpu.VMEM(weights, bf16),
            pltpu.VMEM(weights, bf16),
            pltpu.VMEM((2 * own, book_rows), f32),
            pltpu.VMEM(message, f32),
            pltpu.VMEM(message, f32),
            pltpu.VMEM(message, f32),
            pltpu.VMEM((local_groups, group_count, slot, width), f32),
            pltpu.VMEM((local_groups, group_count, slot, width), f32),
            dma((local_groups, group_count)),
            dma((local_groups, group_count)),
        ]
        + [dma((local_groups, shard_count)) for _ in range(8)]
        + [dma((local_groups, group_count)), dma((local_groups, group_count))],
        compiler_params=pltpu.CompilerParams(
            collective_id=0, has_side_effects=True, vmem_limit_bytes=62 * 1024 * 1024
        ),
    )(outgoing, fine_books)
    fine_grad = jnp.swapaxes(fine_t, 1, 2)
    item_grad = contract(placing, home.reshape(slot_total, width), 0, 0)
    coarse_grad = lax.psum(-contract(onehot, item_grad, 0, 0), ("group", "shard"))
    return (item_grad, fine_grad, coarse_grad)


def solution(mesh):
    placed = (P(("group", "shard"), None), P(("group", "shard")), P(), P("group", "shard", None))
    return jax.shard_map(
        per_device,
        mesh=mesh,
        in_specs=placed,
        out_specs=(P(("group", "shard"), None), P("group", "shard", None), P()),
        check_vma=False,
    )
```

time: 432 us -> 259 us (0.60); the launches traced: 424 us -> 259 us
  matrix products: 153 us -> 4.48 us
  Pallas kernels: 0 us -> 118 us
  waiting for transfers between devices: 169 us -> 114 us
  blocking collectives: 49.3 us -> 0 us
  other arithmetic: 19.8 us -> 1.49 us
  starting transfers between devices: 9.12 us -> 0.04 us
    dot_general x16 -> x5, matrix products: 153 us -> 4.48 us  [contract(): lax.dot_general(former, latter, (((former_dim,), (latter_dim,)), ((), ())...]
    pallas_call x0 -> x1, Pallas kernels: none -> 118 us  [per_device(): pl.pallas_call(functools.partial(kernel, group_count, shard_count, slot,...]
    psum x1 -> x0, waiting for transfers between devices: 39.2 us -> none  [per_device(): quant_sum, denominator = lax.psum((partial_quant, partial_total), 'shard')]
    psum x1 -> x0, blocking collectives: 13.4 us -> none  [per_device(): quant_sum, denominator = lax.psum((partial_quant, partial_total), 'shard')]
    all_to_all x1 -> x0, blocking collectives: 12.2 us -> none  [per_device(): lax.all_to_all(outgoing, 'group', split_axis=1, concat_axis=1, tiled=True)]
    all_gather x1 -> x0, blocking collectives: 11.9 us -> none  [per_device(): lax.all_gather(arrived_mask, 'shard', axis=1, tiled=True)]
    pmax x1 -> x0, blocking collectives: 11.8 us -> none  [per_device(): peak_score = lax.pmax(jnp.max(scores, axis=1), 'shard')]
    reduce_sum x5 -> x1, other arithmetic: 11.7 us -> 0.11 us  [per_device(): vacant = VACANT * (1.0 - jnp.sum(placing, axis=1, keepdims=True))]
  transfers between devices with their start and end apart: 7 -> 1, of which waited for: 4 -> 1; matrix products, arithmetic and copies ran while one was open for 25% -> 2% of each run, Pallas kernels for 0% -> 0%
where the time goes in v1:
time: 259 us
  Pallas kernels  118 us (46%)
  waiting for transfers between devices  114 us (44%)
  between operations  14.1 us (5%)
  local copies, waits for them, and re-layouts  6.85 us (3%)
  matrix products  4.48 us (2%)
    pallas_call x1, Pallas kernels, per_device(): pl.pallas_call(functools.partial(kernel, group_count, shard_count, slot,...  118 us
    psum x1, waiting for transfers between devices, per_device(): lax.psum(-contract(onehot, item_grad, 0, 0), ('group', 'shard'))  114 us
    unnamed x8, local copies, waits for them, and re-layouts  6.85 us
  transfers between devices with their start and end apart: 1, of which 1 were waited for; matrix products, arithmetic and copies ran while one was open for 2% of the time, Pallas kernels for 0%

profile of v1, /device:TPU:1, one launch (start us, length us, event | category | flops | bytes accessed | tf_op | source)
XLA Modules:
  0.0 258.9 jit_solution(8157768666850254911)
XLA Ops:
  7.2 0.0 copy-start
  7.2 0.0 copy-start.2
  7.2 0.0 all-reduce.2.cloned.1.call-start
  7.2 0.7 and_select_fusion.2
  7.9 0.1 fusion
  8.1 0.7 convert_add_fusion
  8.8 0.1 convert_reduce_fusion
  8.9 0.0 copy-done
  8.9 1.2 convolution_subtract_fusion
  10.1 1.0 convolution_add_fusion
  11.1 118.4 %shard_map.67 = (f32[2,4,32,256]{3,2,1,0:T(8,128)}, f32[2,256,2048]{2,1,0:T(8,128)}) custom-call(f32[2,4,32,256]{3,2,1,0:T(8,128)} %bitcast.8, f32[2,2048,256]{2,1,0:T(8,128)} %books.1), custom_call_target="tpu_custom_call" | custom-call | tf_op jit(solution)/shard_map/pallas_call | solution.py:372
  129.4 1.3 fusion.1
  130.7 0.0 copy-done.2
  130.7 0.0 copy-start.1
  130.7 0.9 convolution_negate_fusion
  131.7 0.0 all-reduce.2.cloned.1.call-update
  131.7 5.4 %copy.8 = f32[2,2048,256]{2,1,0:T(8,128)} copy(f32[2,2048,256]{1,2,0:T(8,128)} %bitcast.7) | data formatting | bytes 8388608
  137.0 0.0 copy-done.1
  137.0 113.5 %all-reduce.2.cloned.1.call-done = f32[64,256]{1,0:T(8,128)} async-done(((f32[64,256]{1,0:T(8,128)}), f32[64,256]{1,0:T(8,128)}) %all-reduce.2.cloned.1.call-update) | async-done | bytes 65552 | tf_op jit(solution)/shard_map/psum | solution.py:403
  250.5 1.5 copy.10
  (1 shorter events, 0.0 us)
Async XLA Ops:
  7.2 1.7 copy-start
  7.2 123.5 %copy-start.2 = (s32[128]{0:T(128)S(1)}, s32[128]{0:T(128)}, u32[]{:S(2)}) copy-start(s32[128]{0:T(128)} %param.5) | copy-start | bytes 1540
  7.2 243.4 %all-reduce.2.cloned.1.call-start = ((), (), s32[]{:S(2)}) async-start(), calls=%async_computation | async-start | bytes 131072 | tf_op jit(solution)/shard_map/psum | solution.py:403
  130.7 6.3 %copy-start.1 = (f32[128,256]{1,0:T(8,128)}, f32[128,256]{1,0:T(8,128)S(1)}, u32[]{:S(2)}) copy-start(f32[128,256]{1,0:T(8,128)S(1)} %fusion.1) | copy-start | bytes 393220
Sparse Core Ops, SparseCore 0:
  131.8 118.6 all-reduce.1

commit v2 on v1

--- a/solution.py
+++ b/solution.py
@@ -29,18 +29,19 @@
     return high, (value - high.astype(jnp.float32)).astype(jnp.bfloat16)
 
 
+def widened(left, right, latter_dim):
+    return lax.dot_general(
+        jnp.concatenate(left, axis=1),
+        jnp.concatenate(right, axis=latter_dim),
+        (((1,), (latter_dim,)), ((), ())),
+        preferred_element_type=jnp.float32,
+    )
+
+
 def triple(former, latter, latter_dim):
-    def one(left, right):
-        return lax.dot_general(
-            left,
-            right,
-            (((1,), (latter_dim,)), ((), ())),
-            preferred_element_type=jnp.float32,
-        )
-
-    return (
-        one(former[0], latter[0]) + one(former[0], latter[1]) + one(former[1], latter[0])
-    )
+    left = [former[0], former[0], former[1]]
+    right = [latter[0], latter[1], latter[0]]
+    return widened(left, right, latter_dim)
 
 
 def kernel(
@@ -50,8 +51,10 @@
     chunk,
     outgoing,
     books,
+    chooser,
     home_out,
     fine_t,
+    coarse_out,
     rows,
     book_high,
     book_low,
@@ -63,6 +66,10 @@
     full,
     back,
     home,
+    coarse_part,
+    coarse_in,
+    coarse_mid,
+    coarse_full,
     z_send,
     z_recv,
     ag_send,
@@ -75,6 +82,12 @@
     b_recv,
     h_send,
     h_recv,
+    c_send,
+    c_recv,
+    m_send,
+    m_recv,
+    e_send,
+    e_recv,
 ):
     local_groups, book_rows, width = books.shape
     own = group_count * slot
@@ -132,16 +145,17 @@
             other = shard_peer(offset)
             ag_copy(b, other, s).start()
 
-    @pl.loop(0, book_rows // chunk)
-    def _(step):
-        at = pl.ds(step * chunk, chunk)
-        for b in range(local_groups):
+    def split_book(b):
+        @pl.loop(0, book_rows // chunk)
+        def _(step):
+            at = pl.ds(step * chunk, chunk)
             high, low = halves(books[b, at])
             book_high[b, at] = high
             book_low[b, at] = low
 
     for b in range(local_groups):
         spread_rows(b)
+        split_book(b)
 
     def load_rows(b, at, count):
         value = rows[b, at].reshape(count, width)
@@ -262,7 +276,11 @@
             slope = (high.astype(jnp.float32) + low.astype(jnp.float32)) * (align - inner)
             slope_pair = halves(slope)
             pushed += triple(slope_pair, book(b, step), 0)
-            fine_t[b, :, at] += triple(error_t, (high, low), 0) + triple(entries_t, slope_pair, 0)
+            fine_t[b, :, at] += widened(
+                [error_t[0], error_t[0], error_t[1], entries_t[0], entries_t[0], entries_t[1]],
+                [high, low, high, slope_pair[0], slope_pair[1], slope_pair[0]],
+                0,
+            )
         pushed = sharpness * alpha * pushed
         for core in range(2):
             owner = 2 * tile + core
@@ -320,6 +338,55 @@
         for offset in range(1, group_count):
             h_copy(b, group_peer(offset), group_peer(offset)).wait_recv()
     home_out[...] = home[...]
+
+    local = home[...].reshape(local_groups * own, width)
+    select = chooser[...].astype(jnp.bfloat16)
+    coarse = jnp.zeros((select.shape[0], width), jnp.float32)
+    for _ in range(3):
+        piece = local.astype(jnp.bfloat16)
+        local = local - piece.astype(jnp.float32)
+        coarse -= jnp.dot(select, piece, preferred_element_type=jnp.float32)
+    count = coarse_part.shape[1]
+    for i in range(shard_count):
+        coarse_part[i] = coarse[i * count : (i + 1) * count]
+
+    def c_copy(other, sender):
+        return remote(
+            coarse_part.at[other], coarse_in.at[sender], c_send.at[other], c_recv.at[sender], (g, other)
+        )
+
+    def m_copy(other, block):
+        return remote(
+            coarse_mid.at[block], coarse_mid.at[block], m_send.at[other], m_recv.at[block], (other, s)
+        )
+
+    def e_copy(other, block):
+        return remote(
+            coarse_full.at[block], coarse_full.at[block], e_send.at[other], e_recv.at[block], (g, other)
+        )
+
+    for offset in range(1, shard_count):
+        c_copy(shard_peer(offset), s).start()
+    coarse_in[s] = coarse_part[s]
+    for offset in range(1, shard_count):
+        c_copy(shard_peer(offset), shard_peer(offset)).wait_recv()
+    coarse_mid[g] = jnp.sum(coarse_in[...], axis=0)
+    for offset in range(1, group_count):
+        m_copy(group_peer(offset), g).start()
+    for offset in range(1, group_count):
+        m_copy(group_peer(offset), group_peer(offset)).wait_recv()
+    coarse_full[s] = jnp.sum(coarse_mid[...], axis=0)
+    for offset in range(1, shard_count):
+        e_copy(shard_peer(offset), s).start()
+    for offset in range(1, shard_count):
+        e_copy(shard_peer(offset), shard_peer(offset)).wait_recv()
+    for i in range(shard_count):
+        coarse_out[i * count : (i + 1) * count] = coarse_full[i]
+    for offset in range(1, group_count):
+        m_copy(group_peer(offset), g).wait_send()
+    for offset in range(1, shard_count):
+        c_copy(shard_peer(offset), s).wait_send()
+        e_copy(shard_peer(offset), s).wait_send()
     for b in range(local_groups):
         for offset in range(1, group_count):
             h_copy(b, group_peer(offset), g).wait_send()
@@ -369,14 +436,17 @@
     message = (local_groups, shard_count, own + STAT, width)
     weights = (local_groups, shard_count // 2, 2 * own, book_rows)
     vmem = pl.BlockSpec(memory_space=pltpu.VMEM)
-    home, fine_t = pl.pallas_call(
+    chooser = contract(onehot, placing, 0, 1)
+    part = coarse_total // shard_count
+    home, fine_t, coarse_grad = pl.pallas_call(
         functools.partial(kernel, group_count, shard_count, slot, chunk),
         out_shape=(
             jax.ShapeDtypeStruct((local_groups, group_count, slot, width), f32),
             jax.ShapeDtypeStruct((local_groups, width, book_rows), f32),
+            jax.ShapeDtypeStruct((coarse_total, width), f32),
         ),
-        in_specs=[vmem, vmem],
-        out_specs=(vmem, vmem),
+        in_specs=[vmem, vmem, vmem],
+        out_specs=(vmem, vmem, vmem),
         scratch_shapes=[
             pltpu.VMEM((local_groups, shard_count, own, width), f32),
             pltpu.VMEM((local_groups, book_rows, width), bf16),
@@ -389,18 +459,22 @@
             pltpu.VMEM(message, f32),
             pltpu.VMEM((local_groups, group_count, slot, width), f32),
             pltpu.VMEM((local_groups, group_count, slot, width), f32),
+            pltpu.VMEM((shard_count, part, width), f32),
+            pltpu.VMEM((shard_count, part, width), f32),
+            pltpu.VMEM((group_count, part, width), f32),
+            pltpu.VMEM((shard_count, part, width), f32),
             dma((local_groups, group_count)),
             dma((local_groups, group_count)),
         ]
         + [dma((local_groups, shard_count)) for _ in range(8)]
-        + [dma((local_groups, group_count)), dma((local_groups, group_count))],
+        + [dma((local_groups, group_count)) for _ in range(2)]
+        + [dma((count,)) for count in [shard_count] * 2 + [group_count] * 2 + [shard_count] * 2],
         compiler_params=pltpu.CompilerParams(
             collective_id=0, has_side_effects=True, vmem_limit_bytes=62 * 1024 * 1024
         ),
-    )(outgoing, fine_books)
+    )(outgoing, fine_books, chooser)
     fine_grad = jnp.swapaxes(fine_t, 1, 2)
     item_grad = contract(placing, home.reshape(slot_total, width), 0, 0)
-    coarse_grad = lax.psum(-contract(onehot, item_grad, 0, 0), ("group", "shard"))
     return (item_grad, fine_grad, coarse_grad)
 
 

time: 259 us -> 145 us (0.56)
  waiting for transfers between devices: 114 us -> 0 us
  between operations: 14.1 us -> 0.67 us
  Pallas kernels: 118 us -> 130 us
    psum x1 -> x0, waiting for transfers between devices: 114 us -> none  [per_device(): lax.psum(-contract(onehot, item_grad, 0, 0), ('group', 'shard'))]
    pallas_call x1, Pallas kernels: 118 us -> 130 us  [per_device(): pl.pallas_call(functools.partial(kernel, group_count, shard_count, slot,...]
    unnamed x8 -> x6, local copies, waits for them, and re-layouts: 6.85 us -> 6.02 us
  transfers between devices with their start and end apart: 1 -> 0, of which waited for: 1 -> 0; matrix products, arithmetic and copies ran while one was open for 2% -> 0% of each run, Pallas kernels for 0% -> 0%
where the time goes in v2:
time: 145 us; the launch traced here: 144 us
  Pallas kernels  130 us (90%)
  local copies, waits for them, and re-layouts  6.02 us (4%)
  matrix products  5.74 us (4%)
  other arithmetic  1.5 us (1%)
    pallas_call x1, Pallas kernels, per_device(): pl.pallas_call(functools.partial(kernel, group_count, shard_count, slot,...  130 us
    unnamed x6, local copies, waits for them, and re-layouts  6.02 us
    dot_general x5, matrix products, contract(): lax.dot_general(former, latter, (((former_dim,), (latter_dim,)), ((), ())...  5.74 us

profile of v2, /device:TPU:1, one launch (start us, length us, event | category | flops | bytes accessed | tf_op | source)
XLA Modules:
  0.0 144.3 jit_solution(1219705467164547655)
XLA Ops:
  0.6 0.0 copy-start
  0.6 0.7 and_select_fusion.2
  1.3 0.1 fusion
  1.5 0.7 convert_add_fusion
  2.2 0.1 convert_reduce_fusion
  2.3 1.5 %fusion.2.chooser = f32[64,256]{1,0:T(8,128)} fusion(s32[128]{0:T(128)S(1)} %convert_add_fusion, s32[128]{0:T(128)} %param.5), kind=kOutput, calls=%fused_computation.7 | convolution fusion | flops 4243456 | bytes 66560 | tf_op jit(solution)/shard_map/dot_general | solution.py:18
  3.8 0.0 copy-done
  3.9 1.2 convolution_subtract_fusion
  5.0 1.0 convolution_add_fusion
  6.0 130.3 %shard_map.67 = (f32[2,4,32,256]{3,2,1,0:T(8,128)}, f32[2,256,2048]{2,1,0:T(8,128)}, f32[64,256]{1,0:T(8,128)}) custom-call(f32[2,4,32,256]{3,2,1,0:T(8,128)} %bitcast.7, f32[2,2048,256]{2,1,0:T(8,128)} %books.1, f32[64,256]{1,0:T(8,128)} %fusion.2.chooser), custom_call_target="tpu_custom_call" | custom-call | tf_op jit(solution)/shard_map/pallas_call | solution.py:441
  136.3 1.9 %fusion.1 = f32[128,256]{1,0:T(8,128)} fusion(f32[256,256]{1,0:T(8,128)} %bitcast.8, s32[128]{0:T(128)S(1)} %convert_add_fusion), kind=kOutput, calls=%fused_computation.6 | convolution fusion | flops 100696064 | bytes 393728 | tf_op jit(solution)/shard_map/dot_general | solution.py:18
  138.3 0.0 copy-start.1
  138.3 5.4 %copy.8 = f32[2,2048,256]{2,1,0:T(8,128)} copy(f32[2,2048,256]{1,2,0:T(8,128)} %bitcast.6) | data formatting | bytes 8388608
  143.6 0.0 copy-done.1
  143.6 0.6 copy.10
  (1 shorter events, 0.0 us)
Async XLA Ops:
  0.6 3.2 %copy-start = (f32[64,256]{1,0:T(8,128)S(1)}, f32[64,256]{1,0:T(8,128)}, u32[]{:S(2)}) copy-start(f32[64,256]{1,0:T(8,128)} %param.6) | copy-start | bytes 196612
  138.3 5.4 %copy-start.1 = (f32[64,256]{1,0:T(8,128)S(1)}, f32[64,256]{1,0:T(8,128)}, u32[]{:S(2)}) copy-start(f32[64,256]{1,0:T(8,128)} %get-tuple-element.20) | copy-start | bytes 196612

commit v3 on v2

--- a/solution.py
+++ b/solution.py
@@ -95,6 +95,9 @@
     g = lax.axis_index("group")
     s = lax.axis_index("shard")
     chip = s // 2
+    parity = lax.rem(s, 2)
+    sibling = s + 1 - 2 * parity
+    across = [lax.rem(s + 2 * hop, shard_count) for hop in range(1, chips)]
 
     def shard_peer(offset):
         return lax.rem(s + offset, shard_count)
@@ -138,11 +141,19 @@
             rows.at[b, block], rows.at[b, block], ag_send.at[b, other], ag_recv.at[b, block], (g, other)
         )
 
+    def passing(buffer, send, recv, b, block):
+        return remote(
+            buffer.at[b, block],
+            buffer.at[b, block],
+            send.at[b, block + 1 - 2 * parity],
+            recv.at[b, block],
+            (g, sibling),
+        )
+
     def spread_rows(b):
         for offset in range(1, group_count):
             z_copy(b, group_peer(offset), group_peer(offset)).wait_recv()
-        for offset in range(1, shard_count):
-            other = shard_peer(offset)
+        for other in across + [sibling]:
             ag_copy(b, other, s).start()
 
     def split_book(b):
@@ -189,13 +200,8 @@
 
     def score_tile(b, turn):
         tile = lax.rem(chip + turn, chips)
-        for core in range(2):
-            owner = 2 * tile + core
-
-            @pl.when(owner != s)
-            def _():
-                ag_copy(b, owner, owner).wait_recv()
-
+        other = 2 * tile + 1 - parity
+        ag_copy(b, other, other).wait_recv()
         entries, _ = load_rows(b, pl.ds(2 * tile, 2), 2 * own)
         pair = halves(entries)
         peak = None
@@ -242,18 +248,19 @@
         full[b, s, :own] = value
         line = lax.broadcasted_iota(jnp.int32, (STAT, own), 0)
         full[b, s, own:, :own] = jnp.where(line == 0, peak, 1.0 / total)
-        for offset in range(1, shard_count):
-            f_copy(b, shard_peer(offset), s).start()
+        for other in across + [sibling]:
+            f_copy(b, other, s).start()
 
     def slope_tile(b, turn):
         tile = lax.rem(chip + turn, chips)
+        other = 2 * tile + 1 - parity
+        f_copy(b, other, other).wait_recv()
         columns = []
         for core in range(2):
             owner = 2 * tile + core
 
             @pl.when(owner != s)
             def _():
-                f_copy(b, owner, owner).wait_recv()
                 q_copy(b, owner, s).wait_send()
 
             mine = part_out[b, owner, own:, :own]
@@ -317,16 +324,30 @@
         def _(turn):
             slope_tile(b, turn + 1)
 
+    def pass_rows(b):
+        for block in across:
+            ag_copy(b, block, block).wait_recv()
+            passing(rows, ag_send, ag_recv, b, block).start()
+
+    def pass_full(b):
+        for block in across:
+            f_copy(b, block, block).wait_recv()
+            passing(full, f_send, f_recv, b, block).start()
+
     fine_t[...] = jnp.zeros_like(fine_t)
     half = chips // 2
-    score_tiles(0, 0, chips)
+    score_tiles(0, 0, 1)
+    pass_rows(0)
+    score_tiles(0, 1, chips)
     for b in range(1, local_groups):
+        pass_rows(b)
         score_tiles(b, 0, half)
         combine(b - 1)
         score_tiles(b, half, chips)
     if local_groups == 1:
         combine(0)
     for b in range(local_groups):
+        pass_full(b)
         slope_tiles(b, 0, half)
         if b == 0 and local_groups > 1:
             combine(local_groups - 1)
@@ -392,10 +413,13 @@
             h_copy(b, group_peer(offset), g).wait_send()
             z_copy(b, group_peer(offset), g).wait_send()
         for offset in range(1, shard_count):
-            other = shard_peer(offset)
+            b_copy(b, shard_peer(offset), s).wait_send()
+        for other in across + [sibling]:
             ag_copy(b, other, s).wait_send()
             f_copy(b, other, s).wait_send()
-            b_copy(b, other, s).wait_send()
+        for block in across:
+            passing(rows, ag_send, ag_recv, b, block).wait_send()
+            passing(full, f_send, f_recv, b, block).wait_send()
 
 
 def per_device(vectors, item_codes, coarse_book, fine_books):

time: 145 us -> 135 us (0.931)
  Pallas kernels: 130 us -> 121 us
    pallas_call x1, Pallas kernels: 130 us -> 121 us  [per_device(): pl.pallas_call(functools.partial(kernel, group_count, shard_count, slot,...]
where the time goes in v3:
time: 135 us
  Pallas kernels  121 us (90%)
  local copies, waits for them, and re-layouts  6.02 us (4%)
  matrix products  5.74 us (4%)
  other arithmetic  1.5 us (1%)
    pallas_call x1, Pallas kernels, per_device(): pl.pallas_call(functools.partial(kernel, group_count, shard_count, slot,...  121 us
    unnamed x6, local copies, waits for them, and re-layouts  6.02 us
    dot_general x5, matrix products, contract(): lax.dot_general(former, latter, (((former_dim,), (latter_dim,)), ((), ())...  5.74 us

profile of v3, /device:TPU:1, one launch (start us, length us, event | category | flops | bytes accessed | tf_op | source)
XLA Modules:
  0.0 134.8 jit_solution(4012148807335391330)
XLA Ops:
  0.6 0.0 copy-start
  0.6 0.7 and_select_fusion.2
  1.3 0.1 fusion
  1.5 0.7 convert_add_fusion
  2.2 0.1 convert_reduce_fusion
  2.3 1.5 %fusion.2.chooser = f32[64,256]{1,0:T(8,128)} fusion(s32[128]{0:T(128)S(1)} %convert_add_fusion, s32[128]{0:T(128)} %param.5), kind=kOutput, calls=%fused_computation.7 | convolution fusion | flops 4243456 | bytes 66560 | tf_op jit(solution)/shard_map/dot_general | solution.py:18
  3.8 0.0 copy-done
  3.9 1.2 convolution_subtract_fusion
  5.0 1.0 convolution_add_fusion
  6.0 120.9 %shard_map.67 = (f32[2,4,32,256]{3,2,1,0:T(8,128)}, f32[2,256,2048]{2,1,0:T(8,128)}, f32[64,256]{1,0:T(8,128)}) custom-call(f32[2,4,32,256]{3,2,1,0:T(8,128)} %bitcast.7, f32[2,2048,256]{2,1,0:T(8,128)} %books.1, f32[64,256]{1,0:T(8,128)} %fusion.2.chooser), custom_call_target="tpu_custom_call" | custom-call | tf_op jit(solution)/shard_map/pallas_call | solution.py:465
  126.9 1.9 %fusion.1 = f32[128,256]{1,0:T(8,128)} fusion(f32[256,256]{1,0:T(8,128)} %bitcast.8, s32[128]{0:T(128)S(1)} %convert_add_fusion), kind=kOutput, calls=%fused_computation.6 | convolution fusion | flops 100696064 | bytes 393728 | tf_op jit(solution)/shard_map/dot_general | solution.py:18
  128.8 0.0 copy-start.1
  128.8 5.4 %copy.8 = f32[2,2048,256]{2,1,0:T(8,128)} copy(f32[2,2048,256]{1,2,0:T(8,128)} %bitcast.6) | data formatting | bytes 8388608
  134.2 0.0 copy-done.1
  134.2 0.6 copy.10
  (1 shorter events, 0.0 us)
Async XLA Ops:
  0.6 3.2 %copy-start = (f32[64,256]{1,0:T(8,128)S(1)}, f32[64,256]{1,0:T(8,128)}, u32[]{:S(2)}) copy-start(f32[64,256]{1,0:T(8,128)} %param.6) | copy-start | bytes 196612
  128.8 5.4 %copy-start.1 = (f32[64,256]{1,0:T(8,128)S(1)}, f32[64,256]{1,0:T(8,128)}, u32[]{:S(2)}) copy-start(f32[64,256]{1,0:T(8,128)} %get-tuple-element.20) | copy-start | bytes 196612
